TPU v7x, 32 devices: a whole 2x2x4 slice. The times are simulated.
32 devices in a mesh: dp: 4 (over z), bank: 4 (over y, x), head: 2 (over core).
Axes of the slice: x: 2, y: 2, z: 4, core: 2. Of those that a mesh axis runs over, the one named last changes fastest.
Arguments:
- feats: bfloat16 [2048, 2048], P('dp'), may hold values from -6 to 6
- w_first: bfloat16 [2048, 2048], P(None, ('bank', 'head')), may hold values from -0.125 to 0.125
- w_second: bfloat16 [2048, 256], P(('bank', 'head')), may hold values from -0.125 to 0.125
- fresh_keys: float32 [2048, 256], P('dp'), may hold values from -6 to 6
- bank: float32 [32768, 256], P(('bank', 'head'))
- block_lists: int32 [4, 32], P('dp'), may hold values from 0 to 63, as said below
- dest_rows: int32 [2048], P('dp'), may hold values from 0 to 32767, as said below
Outputs:
- loss: float32 [2048], P('dp')
- grad_first: float32 [2048, 2048], P('dp', ('bank', 'head'))
- grad_second: float32 [2048, 256], P(('bank', 'head'))
- new_bank: float32 [32768, 256], P(('bank', 'head'))
Inputs may be any that keep to these rules, and one draw needn't show every extreme that they name: `block_lists`: each row names 32 different blocks. `dest_rows`: all entries differ; the 512 entries of query block g name exactly 64 rows in each range of rows o * 4096 to (o + 1) * 4096 - 1.
All inputs are finite; a program needn't handle non-finite values.
Results may differ from a plain program's by a relative error of at most 0.012.
Values sent between devices are 32-bit elements; how exact they have to be, the bound alone decides.
A program may use at most 128 MiB of HBM per device.

v0:
```python
import jax
import jax.numpy as jnp
from jax import lax
from jax.sharding import PartitionSpec as P

BLOCK = 512
sharpness_divisor = 0.2
epsilon = 1e-06
lowest = -1e30


def joined(array, axis, combine):
    everything = jax.tree.map(lambda part: lax.all_gather(part, axis), array)
    leading = jax.tree.map(lambda part: part[0], everything)

    def hop(k, so_far):
        return combine(so_far, jax.tree.map(lambda part: part[k], everything))

    return lax.fori_loop(1, lax.axis_size(axis), hop, leading)


def unit_rows(values):
    norms = jnp.sqrt(jnp.sum(values * values, axis=1, keepdims=True) + epsilon)
    return (values / norms, norms)


def exact_scores(anchor_matrix, bank_entries):
    return (
        lax.dot_general(
            anchor_matrix,
            bank_entries,
            (((1,), (1,)), ((), ())),
            precision=lax.Precision.HIGHEST,
            preferred_element_type=jnp.float32,
        )
        / sharpness_divisor
    )


def join_stats(first, second):
    best = jnp.maximum(first[0], second[0])
    partition_total = first[1] * jnp.exp(first[0] - best) + second[1] * jnp.exp(second[0] - best)
    return (best, partition_total)


def shards(feats, w_first, w_second, fresh_keys, bank, block_lists, dest_rows):
    owner = lax.axis_index(("bank", "head"))
    owner_rows = bank.shape[0]
    hidden = jnp.maximum(jnp.dot(feats, w_first, preferred_element_type=jnp.float32), 0.0).astype(
        jnp.bfloat16
    )
    partial_embed = jnp.dot(hidden, w_second, preferred_element_type=jnp.float32)
    embed = lax.psum(partial_embed, ("bank", "head"))
    anchor_matrix, norms = unit_rows(embed)
    unit_length_bank, unused = unit_rows(fresh_keys)
    matching_similarity = jnp.sum(anchor_matrix * unit_length_bank, axis=1) / sharpness_divisor
    listed = block_lists[0]
    blocks_here = owner_rows // BLOCK
    owned = listed // blocks_here == owner
    owned_count = jnp.sum(owned.astype(jnp.int32))
    order = jnp.argsort(jnp.where(owned, 0, 1).astype(jnp.int32), stable=True)
    local_blocks = listed[order] - owner * blocks_here
    row_count = anchor_matrix.shape[0]

    def block_keys(index):
        return lax.dynamic_slice_in_dim(bank, local_blocks[index] * BLOCK, BLOCK, 0)

    start_best = jnp.full((row_count,), lowest, jnp.float32)
    start_total = jnp.zeros((row_count,), jnp.float32)
    start_weighted = jnp.zeros((row_count, anchor_matrix.shape[1]), jnp.float32)

    def first_pass(index, carry):
        best, partition_total = carry
        similarity_matrix = exact_scores(anchor_matrix, block_keys(index))
        new_best = jnp.maximum(best, jnp.max(similarity_matrix, axis=1))
        partition_total = partition_total * jnp.exp(best - new_best) + jnp.sum(
            jnp.exp(similarity_matrix - new_best[:, None]), axis=1
        )
        return (new_best, partition_total)

    local_stats = lax.fori_loop(0, owned_count, first_pass, (start_best, start_total))
    neg_best, neg_total = joined(local_stats, ("bank", "head"), join_stats)
    best = jnp.maximum(neg_best, matching_similarity)
    positive_weight = jnp.exp(matching_similarity - best)
    partition_total = neg_total * jnp.exp(neg_best - best) + positive_weight

    def second_pass(index, probability_mixed_bank):
        bank_entries = block_keys(index)
        shares = (
            jnp.exp(exact_scores(anchor_matrix, bank_entries) - best[:, None])
            / partition_total[:, None]
        )
        return probability_mixed_bank + jnp.dot(
            shares,
            bank_entries,
            precision=lax.Precision.HIGHEST,
            preferred_element_type=jnp.float32,
        )

    local_weighted = lax.fori_loop(0, owned_count, second_pass, start_weighted)
    probability_mixed_bank = lax.psum(local_weighted, ("bank", "head"))
    loss = best + jnp.log(partition_total) - matching_similarity
    anchor_derivative = (
        probability_mixed_bank
        + (positive_weight / partition_total - 1.0)[:, None] * unit_length_bank
    ) / sharpness_divisor
    inner = jnp.sum(anchor_matrix * anchor_derivative, axis=1, keepdims=True)
    grad_z = ((anchor_derivative - anchor_matrix * inner) / norms).astype(jnp.bfloat16)
    second_part = lax.dot_general(
        hidden, grad_z, (((0,), (0,)), ((), ())), preferred_element_type=jnp.float32
    )
    grad_second = lax.psum(second_part, "dp")
    grad_hidden = lax.dot_general(
        grad_z, w_second, (((1,), (1,)), ((), ())), preferred_element_type=jnp.float32
    )
    grad_pre = jnp.where(hidden > 0, grad_hidden, 0.0).astype(jnp.bfloat16)
    grad_first = lax.psum_scatter(
        lax.dot_general(
            feats, grad_pre, (((0,), (0,)), ((), ())), preferred_element_type=jnp.float32
        ),
        "dp",
        scatter_dimension=0,
        tiled=True,
    )
    got_keys, got_dest = (
        lax.all_gather(unit_length_bank, "dp", axis=0, tiled=True),
        lax.all_gather(dest_rows.astype(jnp.float32), "dp", axis=0, tiled=True),
    )
    local_rows = got_dest.astype(jnp.int32) - owner * owner_rows
    inside = (local_rows >= 0) & (local_rows < owner_rows)
    new_bank = bank.at[jnp.where(inside, local_rows, owner_rows)].set(got_keys, mode="drop")
    return (loss, grad_first, grad_second, new_bank)


def solution(mesh):
    return jax.shard_map(
        shards,
        mesh=mesh,
        in_specs=(
            P("dp", None),
            P(None, ("bank", "head")),
            P(("bank", "head"), None),
            P("dp", None),
            P(("bank", "head"), None),
            P("dp", None),
            P("dp"),
        ),
        out_specs=(
            P("dp"),
            P("dp", ("bank", "head")),
            P(("bank", "head"), None),
            P(("bank", "head"), None),
        ),
        check_vma=False,
    )
```

profile of v0, /device:TPU:0, one launch (start us, length us, event | category | flops | bytes accessed | tf_op | source)
XLA Modules:
  0.0 383.6 jit_solution(11246029741084995186)
XLA Ops:
  7.2 4.6 %copy.49 = f32[4096,256]{1,0:T(8,128)} copy(f32[4096,256]{1,0:T(8,128)} %param.17) | data formatting | bytes 8388608
  17.1 54.1 %all-reduce.4.cloned.1.call-done = f32[512,256]{1,0:T(8,128)} async-done(((f32[512,256]{1,0:T(8,128)}), f32[512,256]{1,0:T(8,128)}) %all-reduce.4.cloned.1.call-update) | async-done | bytes 524304 | tf_op jit(solution)/shard_map/psum | solution.py:53
  74.5 36.0 %while.39 = (s32[]{:T(128)}, f32[512]{0:T(512)S(1)}, f32[512]{0:T(512)S(1)}, s32[]{:T(128)}, s32[32]{0:T(128)S(1)}, /*index=5*/f32[4096,256]{1,0:T(8,128)}, f32[...) while((s32[]{:T(128)}, f32[512]{0:T(512)S(1)}, ...), condition=%wide.region_7.8_spmd, body=%wide.region_4.0_spmd.sunk | while | flops 806355968 | bytes 3172573 | solution.py:81
  81.0 2.1 fusion.40
  94.2 2.1 fusion.40
  107.5 2.1 fusion.40
  110.5 7.4 %all-gather.2 = f32[8,1,512]{2,1,0:T(1,128)S(1)} all-gather(f32[1,1,512]{2,1,0:T(1,128)S(1)} %bitcast.49), channel_id=2, replica_groups=mesh['dp'=4,'bank'=4,'head'=2] {'bank','head'}, dimensions={0}, use_global_device_ids=true | all-gather | bytes 18432 | tf_op jit(solution)/shard_map/all_gather | solution.py:13
  118.0 9.4 %all-gather.3 = f32[8,1,512]{2,1,0:T(1,128)S(1)} all-gather(f32[1,1,512]{2,1,0:T(1,128)S(1)} %bitcast.52), channel_id=3, replica_groups=mesh['dp'=4,'bank'=4,'head'=2] {'bank','head'}, dimensions={0}, use_global_device_ids=true | all-gather | bytes 18432 | tf_op jit(solution)/shard_map/all_gather | solution.py:13
  128.4 62.4 %while.41 = (s32[]{:T(128)}, f32[512,256]{1,0:T(8,128)S(1)}, s32[]{:T(128)}, s32[32]{0:T(128)}, f32[4096,256]{1,0:T(8,128)}, /*index=5*/f32[512,256]{1,0:T(8,128...) while((s32[]{:T(128)}, f32[512,256]{1,0:T(8,128)S(1)}, ...), condition=%wide.region_13.14_spmd, body=%wide.region_12.13_spmd.sunk | while | flops 1611530240 | bytes 4722921 | solution.py:100
  130.9 2.2 fusion.45
  133.1 3.0 convolution_add_fusion.2
  138.6 2.2 fusion.45
  140.8 3.0 convolution_add_fusion.2
  146.3 2.2 fusion.45
  148.5 3.0 convolution_add_fusion.2
  154.1 2.2 fusion.45
  156.3 3.0 convolution_add_fusion.2
  161.8 2.2 fusion.45
  164.0 3.0 convolution_add_fusion.2
  169.5 2.2 fusion.45
  171.7 3.0 convolution_add_fusion.2
  177.2 2.2 fusion.45
  179.4 3.0 convolution_add_fusion.2
  184.9 2.2 fusion.45
  187.1 3.0 convolution_add_fusion.2
  192.4 52.9 %all-reduce.6.cloned.1.call-done = f32[512,256]{1,0:T(8,128)} async-done(((f32[512,256]{1,0:T(8,128)}), f32[512,256]{1,0:T(8,128)}) %all-reduce.6.cloned.1.call-update) | async-done | bytes 524304 | tf_op jit(solution)/shard_map/psum | solution.py:101
  248.8 3.3 convolution_bitcast_fusion
  252.8 12.1 %all-gather.4 = f32[4,1,512]{2,1,0:T(1,128)S(1)} all-gather(f32[1,1,512]{2,1,0:T(1,128)S(1)} %bitcast.58), channel_id=1, replica_groups=mesh['dp'=4,'bank'=4,'head'=2] {'dp'}, dimensions={0}, use_global_device_ids=true | all-gather | bytes 10240 | tf_op jit(solution)/shard_map/all_gather | solution.py:127
  265.9 27.0 %all-gather.7.cloned.1.call-done = f32[2048,256]{1,0:T(8,128)} async-done(((f32[512,256]{1,0:T(8,128)}), f32[2048,256]{1,0:T(8,128)}) %all-gather.7.cloned.1.call-update) | async-done | bytes 2097168 | tf_op jit(solution)/shard_map/all_gather | solution.py:126
  292.9 13.6 %scatter_fusion = f32[4096,256]{1,0:T(8,128)} fusion(f32[4096,256]{1,0:T(8,128)} %get-tuple-element.541, s32[2048]{0:T(1024)S(1)} %compare_select_fusion, f32[2048,256]{1,0:T(8,128)} %all-gather.7.cloned.1.call-done), kind=kCustom, calls=%fused_computation.1 | custom fusion | bytes 6299648 | tf_op jit(solution)/shard_map/scatter | solution.py:131
  306.5 31.3 %reduce-scatter.2.cloned.1.call-done = f32[512,256]{0,1:T(8,128)} async-done(((f32[2048,256]{0,1:T(8,128)}), f32[512,256]{0,1:T(8,128)}) %reduce-scatter.2.cloned.1.call-update) | async-done | bytes 524304 | tf_op jit(solution)/shard_map/reduce_scatter | solution.py:117
  339.9 35.6 %all-reduce.8.cloned.1.call-done = f32[256,256]{1,0:T(8,128)} async-done(((f32[256,256]{1,0:T(8,128)}), f32[256,256]{1,0:T(8,128)}) %all-reduce.8.cloned.1.call-update) | async-done | bytes 262160 | tf_op jit(solution)/shard_map/psum | solution.py:112
  (128 shorter events, 47.8 us)
Async XLA Ops:
  7.2 4.7 %copy-start = (bf16[512,2048]{1,0:T(8,128)(2,1)S(1)}, bf16[512,2048]{1,0:T(8,128)(2,1)}, u32[]{:S(2)}) copy-start(bf16[512,2048]{1,0:T(8,128)(2,1)} %param.13) | copy-start | bytes 6291460
  7.2 64.1 %all-reduce.4.cloned.1.call-start = ((), (), s32[]{:S(2)}) async-start(), calls=%async_computation.1 | async-start | bytes 1048576 | tf_op jit(solution)/shard_map/psum | solution.py:53
  7.2 4.6 %copy-start.9 = (bf16[2048,256]{1,0:T(8,128)(2,1)S(1)}, bf16[2048,256]{1,0:T(8,128)(2,1)}, u32[]{:S(2)}) copy-start(bf16[2048,256]{1,0:T(8,128)(2,1)} %param.14) | copy-start | bytes 3145732
  11.9 0.9 copy-start.6
  11.9 2.0 copy-start.1
  11.9 5.1 %copy-start.5 = (f32[512,256]{1,0:T(8,128)S(1)}, f32[512,256]{1,0:T(8,128)}, u32[]{:S(2)}) copy-start(f32[512,256]{1,0:T(8,128)} %param.16) | copy-start | bytes 1572868
  13.8 231.5 %all-reduce.6.cloned.1.call-start = ((), (), s32[]{:S(2)}) async-start(), calls=%async_computation.2 | async-start | bytes 1048576 | tf_op jit(solution)/shard_map/psum | solution.py:101
  110.5 17.2 %copy-start.8 = (s32[32]{0:T(128)}, s32[32]{0:T(128)S(1)}, u32[]{:S(2)}) copy-start(s32[32]{0:T(128)S(1)} %get-tuple-element.559) | copy-start | bytes 388
  190.8 0.8 copy-start.2
  191.6 55.2 %copy-start.3 = (f32[512,256]{1,0:T(8,128)S(1)}, f32[512,256]{1,0:T(8,128)}, u32[]{:S(2)}) copy-start(f32[512,256]{1,0:T(8,128)} %get-tuple-element.283) | copy-start | bytes 1572868
  191.6 101.3 %all-gather.7.cloned.1.call-start = ((), (), s32[]{:S(2)}) async-start(), calls=%async_computation.5 | async-start | bytes 2621440 | tf_op jit(solution)/shard_map/all_gather | solution.py:126
  192.4 145.5 %reduce-scatter.2.cloned.1.call-start = ((), (), s32[]{:S(2)}) async-start(), calls=%async_computation.3 | async-start | bytes 2621440 | tf_op jit(solution)/shard_map/reduce_scatter | solution.py:117
  252.1 0.7 copy-start.7
  252.1 12.8 %copy-start.4 = (bf16[512,256]{1,0:T(8,128)(2,1)S(1)}, bf16[512,256]{1,0:T(8,128)(2,1)}, u32[]{:S(2)}) copy-start(bf16[512,256]{1,0:T(8,128)(2,1)} %divide_convert_fusion) | copy-start | bytes 786436
  252.2 123.3 %all-reduce.8.cloned.1.call-start = ((), (), s32[]{:S(2)}) async-start(), calls=%async_computation.4 | async-start | bytes 524288 | tf_op jit(solution)/shard_map/psum | solution.py:112
Sparse Core Ops, SparseCore 0:
  13.9 57.2 all-reduce.3
  191.8 53.5 all-reduce.5
  247.5 45.3 all-gather.6
  295.1 42.7 reduce-scatter.1
  340.7 34.6 all-reduce.7
where the time goes:
time: 386 us; the launch traced here: 384 us
  waiting for transfers between devices  202 us (52%)
  matrix products  64.2 us (17%)
  local copies, waits for them, and re-layouts  39.8 us (10%)
  blocking collectives  28.9 us (7%)
  loops' own time  23.3 us (6%)
  between operations  14 us (4%)
  other arithmetic  11.7 us (3%)
    psum x1, waiting for transfers between devices, shards(): embed = lax.psum(partial_embed, ('bank', 'head'))  54.1 us
    psum x1, waiting for transfers between devices, shards(): probability_mixed_bank = lax.psum(local_weighted, ('bank', 'head'))  52.9 us
    psum x1, waiting for transfers between devices, shards(): grad_second = lax.psum(second_part, 'dp')  35.6 us
    dot_general x16, matrix products, exact_scores(): lax.dot_general(anchor_matrix, bank_entries, (((1,), (1,)), ((), ())), pr...  34.4 us
    reduce_scatter x1, waiting for transfers between devices, shards(): lax.psum_scatter(lax.dot_general(feats, grad_pre, (((0,), (0,)), ((), ())...  31.3 us
    all_gather x1, waiting for transfers between devices, shards(): lax.all_gather(unit_length_bank, 'dp', axis=0, tiled=True)  27 us
    dot_general x8, matrix products, second_pass(): jnp.dot(shares, bank_entries, precision=lax.Precision.HIGHEST, preferred_...  23.8 us
    all_gather x2, blocking collectives, joined(): everything = jax.tree.map(lambda part: lax.all_gather(part, axis), array)  16.8 us
  transfers between devices with their start and end apart: 5, of which 5 were waited for; matrix products, arithmetic and copies ran while one was open for 7% of the time, Pallas kernels for 0%

commit v1 on v0

--- a/solution.py
+++ b/solution.py
@@ -50,7 +50,9 @@
         jnp.bfloat16
     )
     partial_embed = jnp.dot(hidden, w_second, preferred_element_type=jnp.float32)
-    embed = lax.psum(partial_embed, ("bank", "head"))
+    embed = partial_embed
+    for name in ("head", "bank"):
+        embed = lax.psum(embed, name)
     anchor_matrix, norms = unit_rows(embed)
     unit_length_bank, unused = unit_rows(fresh_keys)
     matching_similarity = jnp.sum(anchor_matrix * unit_length_bank, axis=1) / sharpness_divisor

time: 386 us -> 400 us (1.036)
  waiting for transfers between devices: 202 us -> 215 us
    psum x1 -> x2, waiting for transfers between devices: 54.1 us -> 68 us  [shards(): embed = lax.psum(embed, name)]
  transfers between devices with their start and end apart: 5 -> 6, of which waited for: 5 -> 6; matrix products, arithmetic and copies ran while one was open for 7% -> 7% of each run, Pallas kernels for 0% -> 0%
where the time goes in v1:
time: 400 us; the launch traced here: 398 us
  waiting for transfers between devices  215 us (54%)
  matrix products  64.1 us (16%)
  local copies, waits for them, and re-layouts  39.8 us (10%)
  blocking collectives  28.8 us (7%)
  loops' own time  23.3 us (6%)
  between operations  14.3 us (4%)
  other arithmetic  11.8 us (3%)
    psum x2, waiting for transfers between devices, shards(): embed = lax.psum(embed, name)  68 us
    psum x1, waiting for transfers between devices, shards(): probability_mixed_bank = lax.psum(local_weighted, ('bank', 'head'))  53.2 us
    psum x1, waiting for transfers between devices, shards(): grad_second = lax.psum(second_part, 'dp')  35.5 us
    dot_general x16, matrix products, exact_scores(): lax.dot_general(anchor_matrix, bank_entries, (((1,), (1,)), ((), ())), pr...  34.3 us
    reduce_scatter x1, waiting for transfers between devices, shards(): lax.psum_scatter(lax.dot_general(feats, grad_pre, (((0,), (0,)), ((), ())...  31.2 us
    all_gather x1, waiting for transfers between devices, shards(): lax.all_gather(unit_length_bank, 'dp', axis=0, tiled=True)  26.8 us
    dot_general x8, matrix products, second_pass(): jnp.dot(shares, bank_entries, precision=lax.Precision.HIGHEST, preferred_...  23.8 us
    all_gather x2, blocking collectives, joined(): everything = jax.tree.map(lambda part: lax.all_gather(part, axis), array)  16.8 us
  transfers between devices with their start and end apart: 6, of which 6 were waited for; matrix products, arithmetic and copies ran while one was open for 7% of the time, Pallas kernels for 0%

profile of v1, /device:TPU:0, one launch (start us, length us, event | category | flops | bytes accessed | tf_op | source)
XLA Modules:
  0.0 397.8 jit_solution(18245808857279872914)
XLA Ops:
  7.2 4.6 %copy.50 = f32[4096,256]{1,0:T(8,128)} copy(f32[4096,256]{1,0:T(8,128)} %param.17) | data formatting | bytes 8388608
  16.3 19.1 %all-reduce.5.cloned.1.call-done = f32[512,256]{1,0:T(8,128)} async-done(((f32[512,256]{1,0:T(8,128)}), f32[512,256]{1,0:T(8,128)}) %all-reduce.5.cloned.1.call-update) | async-done | bytes 524304 | tf_op jit(solution)/shard_map/psum | solution.py:55
  36.4 48.9 %all-reduce.7.cloned.1.call-done = f32[512,256]{1,0:T(8,128)} async-done(((f32[512,256]{1,0:T(8,128)}), f32[512,256]{1,0:T(8,128)}) %all-reduce.7.cloned.1.call-update) | async-done | bytes 524304 | tf_op jit(solution)/shard_map/psum | solution.py:55
  88.5 36.0 %while.39 = (s32[]{:T(128)}, f32[512]{0:T(512)S(1)}, f32[512]{0:T(512)S(1)}, s32[]{:T(128)}, s32[32]{0:T(128)S(1)}, /*index=5*/f32[4096,256]{1,0:T(8,128)}, f32[...) while((s32[]{:T(128)}, f32[512]{0:T(512)S(1)}, ...), condition=%wide.region_8.9_spmd, body=%wide.region_5.0_spmd.sunk | while | flops 806355968 | bytes 3172573 | solution.py:83
  95.0 2.1 fusion.40
  117.1 2.1 fusion.40
  124.6 7.4 %all-gather.2 = f32[8,1,512]{2,1,0:T(1,128)S(1)} all-gather(f32[1,1,512]{2,1,0:T(1,128)S(1)} %bitcast.49), channel_id=2, replica_groups=mesh['dp'=4,'bank'=4,'head'=2] {'bank','head'}, dimensions={0}, use_global_device_ids=true | all-gather | bytes 18432 | tf_op jit(solution)/shard_map/all_gather | solution.py:13
  132.0 9.4 %all-gather.3 = f32[8,1,512]{2,1,0:T(1,128)S(1)} all-gather(f32[1,1,512]{2,1,0:T(1,128)S(1)} %bitcast.52), channel_id=3, replica_groups=mesh['dp'=4,'bank'=4,'head'=2] {'bank','head'}, dimensions={0}, use_global_device_ids=true | all-gather | bytes 18432 | tf_op jit(solution)/shard_map/all_gather | solution.py:13
  142.4 62.4 %while.41 = (s32[]{:T(128)}, f32[512,256]{1,0:T(8,128)S(1)}, s32[]{:T(128)}, s32[32]{0:T(128)}, f32[4096,256]{1,0:T(8,128)}, /*index=5*/f32[512,256]{1,0:T(8,128...) while((s32[]{:T(128)}, f32[512,256]{1,0:T(8,128)S(1)}, ...), condition=%wide.region_14.15_spmd, body=%wide.region_13.14_spmd.sunk | while | flops 1611530240 | bytes 4722921 | solution.py:102
  144.9 2.2 fusion.45
  147.1 3.0 convolution_add_fusion.2
  152.6 2.2 fusion.45
  154.8 3.0 convolution_add_fusion.2
  160.4 2.2 fusion.45
  162.6 3.0 convolution_add_fusion.2
  168.1 2.2 fusion.45
  170.3 3.0 convolution_add_fusion.2
  175.8 2.2 fusion.45
  178.0 3.0 convolution_add_fusion.2
  183.5 2.2 fusion.45
  185.7 3.0 convolution_add_fusion.2
  191.2 2.2 fusion.45
  193.4 3.0 convolution_add_fusion.2
  198.9 2.2 fusion.45
  201.1 3.0 convolution_add_fusion.2
  206.3 53.2 %all-reduce.9.cloned.1.call-done = f32[512,256]{1,0:T(8,128)} async-done(((f32[512,256]{1,0:T(8,128)}), f32[512,256]{1,0:T(8,128)}) %all-reduce.9.cloned.1.call-update) | async-done | bytes 524304 | tf_op jit(solution)/shard_map/psum | solution.py:103
  262.9 3.3 convolution_bitcast_fusion
  266.9 12.1 %all-gather.4 = f32[4,1,512]{2,1,0:T(1,128)S(1)} all-gather(f32[1,1,512]{2,1,0:T(1,128)S(1)} %bitcast.58), channel_id=1, replica_groups=mesh['dp'=4,'bank'=4,'head'=2] {'dp'}, dimensions={0}, use_global_device_ids=true | all-gather | bytes 10240 | tf_op jit(solution)/shard_map/all_gather | solution.py:129
  280.0 26.8 %all-gather.7.cloned.1.call-done = f32[2048,256]{1,0:T(8,128)} async-done(((f32[512,256]{1,0:T(8,128)}), f32[2048,256]{1,0:T(8,128)}) %all-gather.7.cloned.1.call-update) | async-done | bytes 2097168 | tf_op jit(solution)/shard_map/all_gather | solution.py:128
  306.9 13.6 %scatter_fusion = f32[4096,256]{1,0:T(8,128)} fusion(f32[4096,256]{1,0:T(8,128)} %get-tuple-element.542, s32[2048]{0:T(1024)S(1)} %compare_select_fusion, f32[2048,256]{1,0:T(8,128)} %all-gather.7.cloned.1.call-done), kind=kCustom, calls=%fused_computation.1 | custom fusion | bytes 6299648 | tf_op jit(solution)/shard_map/scatter | solution.py:133
  320.5 31.2 %reduce-scatter.2.cloned.1.call-done = f32[512,256]{0,1:T(8,128)} async-done(((f32[2048,256]{0,1:T(8,128)}), f32[512,256]{0,1:T(8,128)}) %reduce-scatter.2.cloned.1.call-update) | async-done | bytes 524304 | tf_op jit(solution)/shard_map/reduce_scatter | solution.py:119
  353.7 35.5 %all-reduce.11.cloned.1.call-done = f32[256,256]{1,0:T(8,128)} async-done(((f32[256,256]{1,0:T(8,128)}), f32[256,256]{1,0:T(8,128)}) %all-reduce.11.cloned.1.call-update) | async-done | bytes 262160 | tf_op jit(solution)/shard_map/psum | solution.py:114
  (131 shorter events, 49.9 us)
Async XLA Ops:
  7.2 4.7 %copy-start = (bf16[512,2048]{1,0:T(8,128)(2,1)S(1)}, bf16[512,2048]{1,0:T(8,128)(2,1)}, u32[]{:S(2)}) copy-start(bf16[512,2048]{1,0:T(8,128)(2,1)} %param.13) | copy-start | bytes 6291460
  7.2 28.3 %all-reduce.5.cloned.1.call-start = ((), (), s32[]{:S(2)}) async-start(), calls=%async_computation.1 | async-start | bytes 1048576 | tf_op jit(solution)/shard_map/psum | solution.py:55
  7.2 4.6 %copy-start.9 = (bf16[2048,256]{1,0:T(8,128)(2,1)S(1)}, bf16[2048,256]{1,0:T(8,128)(2,1)}, u32[]{:S(2)}) copy-start(bf16[2048,256]{1,0:T(8,128)(2,1)} %param.14) | copy-start | bytes 3145732
  11.9 0.9 copy-start.6
  11.9 2.0 copy-start.1
  12.8 22.7 %copy-start.5 = (f32[512,256]{1,0:T(8,128)S(1)}, f32[512,256]{1,0:T(8,128)}, u32[]{:S(2)}) copy-start(f32[512,256]{1,0:T(8,128)} %param.16) | copy-start | bytes 1572868
  13.8 71.4 %all-reduce.7.cloned.1.call-start = ((), (), s32[]{:S(2)}) async-start(), calls=%async_computation.2 | async-start | bytes 1048576 | tf_op jit(solution)/shard_map/psum | solution.py:55
  35.5 224.0 %all-reduce.9.cloned.1.call-start = ((), (), s32[]{:S(2)}) async-start(), calls=%async_computation.3 | async-start | bytes 1048576 | tf_op jit(solution)/shard_map/psum | solution.py:103
  124.5 17.2 %copy-start.8 = (s32[32]{0:T(128)}, s32[32]{0:T(128)S(1)}, u32[]{:S(2)}) copy-start(s32[32]{0:T(128)S(1)} %get-tuple-element.563) | copy-start | bytes 388
  204.8 0.8 copy-start.2
  205.7 55.2 %copy-start.3 = (f32[512,256]{1,0:T(8,128)S(1)}, f32[512,256]{1,0:T(8,128)}, u32[]{:S(2)}) copy-start(f32[512,256]{1,0:T(8,128)} %get-tuple-element.283) | copy-start | bytes 1572868
  205.7 101.2 %all-gather.7.cloned.1.call-start = ((), (), s32[]{:S(2)}) async-start(), calls=%async_computation.6 | async-start | bytes 2621440 | tf_op jit(solution)/shard_map/all_gather | solution.py:128
  206.2 145.4 %reduce-scatter.2.cloned.1.call-start = ((), (), s32[]{:S(2)}) async-start(), calls=%async_computation.4 | async-start | bytes 2621440 | tf_op jit(solution)/shard_map/reduce_scatter | solution.py:119
  266.2 0.7 copy-start.7
  266.2 12.7 %copy-start.4 = (bf16[512,256]{1,0:T(8,128)(2,1)S(1)}, bf16[512,256]{1,0:T(8,128)(2,1)}, u32[]{:S(2)}) copy-start(bf16[512,256]{1,0:T(8,128)(2,1)} %divide_convert_fusion) | copy-start | bytes 786436
  266.3 123.0 %all-reduce.11.cloned.1.call-start = ((), (), s32[]{:S(2)}) async-start(), calls=%async_computation.5 | async-start | bytes 524288 | tf_op jit(solution)/shard_map/psum | solution.py:114
Sparse Core Ops, SparseCore 0:
  13.9 21.4 all-reduce.4
  38.7 46.5 all-reduce.6
  205.8 53.6 all-reduce.8
  261.5 45.3 all-gather.6
  309.0 42.6 reduce-scatter.1
  354.6 34.6 all-reduce.10
